TPU v7x, 32 devices: a whole 2x2x4 slice. The times are simulated.
32 devices in a mesh: section: 8 (over y, x, core), blk: 4 (over z).
Axes of the slice: x: 2, y: 2, z: 4, core: 2. Of those that a mesh axis runs over, the one named last changes fastest.
Arguments:
- images: bfloat16 [64, 65536], P('section', 'blk'), may hold values from 0 to 1
- tile_weights: bfloat16 [8, 512, 4, 128, 128], P('section', 'blk'), may hold values from -0.5 to 0.5
- tile_columns: int32 [8, 512, 4], P('section', 'blk'), may hold values from 0 to 511, as said below
- tile_counts: int32 [8, 512], P('section', 'blk'), may hold values from 1 to 4
- bias: float32 [8, 65536], P('section', 'blk'), may hold values from -0.3 to 0.3
Outputs:
- features: bfloat16 [64, 65536], P('section', 'blk')
Inputs may be any that keep to these rules, and one draw needn't show every extreme that they name: `tile_columns`: the column block of every tile differs cyclically (modulo 512) from its row block by at most 64 blocks, and a distance of exactly 64 occurs in every layer on both sides.
All inputs are finite; a program needn't handle non-finite values.
Results may differ from a plain program's by a relative error of at most 0.013.
Values may be sent and summed in bfloat16 or wider, within the bound.
A program may use at most 64 MiB of HBM per device.

v0:
```python
import jax
import jax.numpy as jnp
from jax import lax
from jax.sharding import PartitionSpec as P


def extended_2(value, sides, width):
    for axis, dim in sides:
        devices, length = (lax.axis_size(axis), value.shape[dim])
        up = [(i, (i + 1) % devices) for i in range(devices)]
        down = [(j, i) for i, j in up]
        last = lax.slice_in_dim(value, length - width, length, axis=dim)
        first = lax.slice_in_dim(value, 0, width, axis=dim)
        before = lax.ppermute(last, axis, up)
        after = lax.ppermute(first, axis, down)
        value = jnp.concatenate([before, value, after], axis=dim)
    return value


def shifted(value, axis, by):
    devices = lax.axis_size(axis)
    return lax.ppermute(value, axis, [(i, (i + by) % devices) for i in range(devices)])


def shards(images, tile_weights, tile_columns, tile_counts, bias):
    sections = lax.axis_size("section")
    section_index = lax.axis_index("section")
    image_rows = images.shape[0]
    blk_dev = tile_weights.shape[1]
    slots = tile_weights.shape[2]
    tile_size = tile_weights.shape[3]
    shard_width = blk_dev * tile_size
    total_blocks = blk_dev * lax.axis_size("blk")
    first_block = lax.axis_index("blk") * blk_dev
    row_ids = first_block + jnp.arange(blk_dev, dtype=jnp.int32)
    half_blocks = total_blocks // 2
    offset_blocks = (tile_columns[0] - row_ids[:, None] + half_blocks) % total_blocks - half_blocks
    located = jnp.arange(blk_dev, dtype=jnp.int32)[:, None] + offset_blocks + blk_dev
    live_tiles = jnp.arange(slots, dtype=jnp.int32)[None, :] < tile_counts[0][:, None]
    weights = tile_weights[0]
    layer_bias = bias[0]

    def apply_layer(buffer):
        extended = extended_2(buffer, (("blk", 1),), blk_dev * tile_size)
        column_blocks = extended.reshape(image_rows, -1, tile_size)
        selected = column_blocks[:, located, :]
        selected = jnp.where(live_tiles[None, :, :, None], selected, jnp.zeros_like(selected))
        totals = jnp.einsum("irkb,rkba->ira", selected, weights, preferred_element_type=jnp.float32)
        summed = totals.reshape(image_rows, shard_width) + layer_bias[None, :]
        return jnp.clip(summed, 0.0, 32.0).astype(jnp.bfloat16)

    def advance(step_index, buffer):
        anchor = (section_index - step_index) % sections
        entry_tick = (sections - anchor) % sections
        active = jnp.logical_and(step_index >= entry_tick, step_index < entry_tick + sections)
        computed = apply_layer(buffer)
        updated = jnp.where(active, computed, buffer)
        return shifted(updated, "section", 1)

    return lax.fori_loop(0, 2 * sections, advance, images)


def solution(mesh):
    placed = (
        P("section", "blk"),
        P("section", "blk", None, None, None),
        P("section", "blk", None),
        P("section", "blk"),
        P("section", "blk"),
    )
    return jax.shard_map(
        shards, mesh=mesh, in_specs=placed, out_specs=P("section", "blk"), check_vma=False
    )
```

profile of v0, /device:TPU:7, one launch (start us, length us, event | category | flops | bytes accessed | tf_op | source)
XLA Modules:
  0.0 459.0 jit_solution(9139099391624232339)
XLA Ops:
  1.9 456.4 %while.16 = (s32[]{:T(128)}, bf16[8,16384]{1,0:T(8,128)(2,1)S(1)}, s32[]{:T(128)}, s32[128,4]{1,0:T(8,128)S(1)}, bf16[128,4,128,128]{3,2,1,0:T(8,128)(2,1)}, /*i...) while((s32[]{:T(128)}, bf16[8,16384]{1,0:T(8,128)(2,1)S(1)}, ...), condition=%wide.region_1.2_spmd.clone, body=%wide.region_0.1_spmd.clone.sunk | while | flops 137628704 | bytes 25511956 | solution.py:60
  10.3 6.4 %collective-permute-done.1 = bf16[8,16384]{1,0:T(8,128)(2,1)S(1)} collective-permute-done((bf16[8,16384]{1,0:T(8,128)(2,1)S(1)}, bf16[8,16384]{1,0:T(8,128)(2,1)S(1)}, u32[]{:S(2)}, u32[]{:S(2)}) %collective-permute-start.1) | collective-permute-done | bytes 262176 | tf_op jit(solution)/shard_map/while/body/eval_jaxpr/ppermute | solution.py:14
  18.6 7.2 %fusion.22 = bf16[8,16384]{1,0:T(8,128)(2,1)S(1)} fusion(bf16[8,16384]{1,0:T(8,128)(2,1)S(1)} %get-tuple-element.269, bf16[128,4,128,128]{3,2,1,0:T(8,128)(2,1)} %get-tuple-element.283, bf16[128,4,8,128]{3,2,1,0:T(8,128)(2,1)S(1)} %bitcast.52, pred[128,4]{1,0:T(8,128)(4,1)S(1)} %iota_compare_fusion.2, f32[16384]{0:T(1024)S(1)} %bitcast.53, pred[]{:T(512)S(6)} %and.50), kind=kOutput, calls=%fused_computation.6.clone.1 | convolution fusion | flops 135266304 | bytes 18416128 | tf_op jit(solution)/shard_map/while/body/eval_jaxpr/irkb,rkba->ira/dot_general | solution.py:48
  36.1 6.4 %collective-permute-done.1 = bf16[8,16384]{1,0:T(8,128)(2,1)S(1)} collective-permute-done((bf16[8,16384]{1,0:T(8,128)(2,1)S(1)}, bf16[8,16384]{1,0:T(8,128)(2,1)S(1)}, u32[]{:S(2)}, u32[]{:S(2)}) %collective-permute-start.1) | collective-permute-done | bytes 262176 | tf_op jit(solution)/shard_map/while/body/eval_jaxpr/ppermute | solution.py:14
  44.3 7.2 %fusion.22 = bf16[8,16384]{1,0:T(8,128)(2,1)S(1)} fusion(bf16[8,16384]{1,0:T(8,128)(2,1)S(1)} %get-tuple-element.269, bf16[128,4,128,128]{3,2,1,0:T(8,128)(2,1)} %get-tuple-element.283, bf16[128,4,8,128]{3,2,1,0:T(8,128)(2,1)S(1)} %bitcast.52, pred[128,4]{1,0:T(8,128)(4,1)S(1)} %iota_compare_fusion.2, f32[16384]{0:T(1024)S(1)} %bitcast.53, pred[]{:T(512)S(6)} %and.50), kind=kOutput, calls=%fused_computation.6.clone.1 | convolution fusion | flops 135266304 | bytes 18416128 | tf_op jit(solution)/shard_map/while/body/eval_jaxpr/irkb,rkba->ira/dot_general | solution.py:48
  65.4 7.5 %collective-permute-done.1 = bf16[8,16384]{1,0:T(8,128)(2,1)S(1)} collective-permute-done((bf16[8,16384]{1,0:T(8,128)(2,1)S(1)}, bf16[8,16384]{1,0:T(8,128)(2,1)S(1)}, u32[]{:S(2)}, u32[]{:S(2)}) %collective-permute-start.1) | collective-permute-done | bytes 262176 | tf_op jit(solution)/shard_map/while/body/eval_jaxpr/ppermute | solution.py:14
  74.7 7.2 %fusion.22 = bf16[8,16384]{1,0:T(8,128)(2,1)S(1)} fusion(bf16[8,16384]{1,0:T(8,128)(2,1)S(1)} %get-tuple-element.269, bf16[128,4,128,128]{3,2,1,0:T(8,128)(2,1)} %get-tuple-element.283, bf16[128,4,8,128]{3,2,1,0:T(8,128)(2,1)S(1)} %bitcast.52, pred[128,4]{1,0:T(8,128)(4,1)S(1)} %iota_compare_fusion.2, f32[16384]{0:T(1024)S(1)} %bitcast.53, pred[]{:T(512)S(6)} %and.50), kind=kOutput, calls=%fused_computation.6.clone.1 | convolution fusion | flops 135266304 | bytes 18416128 | tf_op jit(solution)/shard_map/while/body/eval_jaxpr/irkb,rkba->ira/dot_general | solution.py:48
  95.1 5.9 %collective-permute-done.1 = bf16[8,16384]{1,0:T(8,128)(2,1)S(1)} collective-permute-done((bf16[8,16384]{1,0:T(8,128)(2,1)S(1)}, bf16[8,16384]{1,0:T(8,128)(2,1)S(1)}, u32[]{:S(2)}, u32[]{:S(2)}) %collective-permute-start.1) | collective-permute-done | bytes 262176 | tf_op jit(solution)/shard_map/while/body/eval_jaxpr/ppermute | solution.py:14
  102.9 7.2 %fusion.22 = bf16[8,16384]{1,0:T(8,128)(2,1)S(1)} fusion(bf16[8,16384]{1,0:T(8,128)(2,1)S(1)} %get-tuple-element.269, bf16[128,4,128,128]{3,2,1,0:T(8,128)(2,1)} %get-tuple-element.283, bf16[128,4,8,128]{3,2,1,0:T(8,128)(2,1)S(1)} %bitcast.52, pred[128,4]{1,0:T(8,128)(4,1)S(1)} %iota_compare_fusion.2, f32[16384]{0:T(1024)S(1)} %bitcast.53, pred[]{:T(512)S(6)} %and.50), kind=kOutput, calls=%fused_computation.6.clone.1 | convolution fusion | flops 135266304 | bytes 18416128 | tf_op jit(solution)/shard_map/while/body/eval_jaxpr/irkb,rkba->ira/dot_general | solution.py:48
  123.3 6.4 %collective-permute-done.1 = bf16[8,16384]{1,0:T(8,128)(2,1)S(1)} collective-permute-done((bf16[8,16384]{1,0:T(8,128)(2,1)S(1)}, bf16[8,16384]{1,0:T(8,128)(2,1)S(1)}, u32[]{:S(2)}, u32[]{:S(2)}) %collective-permute-start.1) | collective-permute-done | bytes 262176 | tf_op jit(solution)/shard_map/while/body/eval_jaxpr/ppermute | solution.py:14
  131.7 7.2 %fusion.22 = bf16[8,16384]{1,0:T(8,128)(2,1)S(1)} fusion(bf16[8,16384]{1,0:T(8,128)(2,1)S(1)} %get-tuple-element.269, bf16[128,4,128,128]{3,2,1,0:T(8,128)(2,1)} %get-tuple-element.283, bf16[128,4,8,128]{3,2,1,0:T(8,128)(2,1)S(1)} %bitcast.52, pred[128,4]{1,0:T(8,128)(4,1)S(1)} %iota_compare_fusion.2, f32[16384]{0:T(1024)S(1)} %bitcast.53, pred[]{:T(512)S(6)} %and.50), kind=kOutput, calls=%fused_computation.6.clone.1 | convolution fusion | flops 135266304 | bytes 18416128 | tf_op jit(solution)/shard_map/while/body/eval_jaxpr/irkb,rkba->ira/dot_general | solution.py:48
  149.9 6.7 %collective-permute-done.1 = bf16[8,16384]{1,0:T(8,128)(2,1)S(1)} collective-permute-done((bf16[8,16384]{1,0:T(8,128)(2,1)S(1)}, bf16[8,16384]{1,0:T(8,128)(2,1)S(1)}, u32[]{:S(2)}, u32[]{:S(2)}) %collective-permute-start.1) | collective-permute-done | bytes 262176 | tf_op jit(solution)/shard_map/while/body/eval_jaxpr/ppermute | solution.py:14
  158.5 7.2 %fusion.22 = bf16[8,16384]{1,0:T(8,128)(2,1)S(1)} fusion(bf16[8,16384]{1,0:T(8,128)(2,1)S(1)} %get-tuple-element.269, bf16[128,4,128,128]{3,2,1,0:T(8,128)(2,1)} %get-tuple-element.283, bf16[128,4,8,128]{3,2,1,0:T(8,128)(2,1)S(1)} %bitcast.52, pred[128,4]{1,0:T(8,128)(4,1)S(1)} %iota_compare_fusion.2, f32[16384]{0:T(1024)S(1)} %bitcast.53, pred[]{:T(512)S(6)} %and.50), kind=kOutput, calls=%fused_computation.6.clone.1 | convolution fusion | flops 135266304 | bytes 18416128 | tf_op jit(solution)/shard_map/while/body/eval_jaxpr/irkb,rkba->ira/dot_general | solution.py:48
  180.2 5.9 %collective-permute-done.1 = bf16[8,16384]{1,0:T(8,128)(2,1)S(1)} collective-permute-done((bf16[8,16384]{1,0:T(8,128)(2,1)S(1)}, bf16[8,16384]{1,0:T(8,128)(2,1)S(1)}, u32[]{:S(2)}, u32[]{:S(2)}) %collective-permute-start.1) | collective-permute-done | bytes 262176 | tf_op jit(solution)/shard_map/while/body/eval_jaxpr/ppermute | solution.py:14
  188.0 7.2 %fusion.22 = bf16[8,16384]{1,0:T(8,128)(2,1)S(1)} fusion(bf16[8,16384]{1,0:T(8,128)(2,1)S(1)} %get-tuple-element.269, bf16[128,4,128,128]{3,2,1,0:T(8,128)(2,1)} %get-tuple-element.283, bf16[128,4,8,128]{3,2,1,0:T(8,128)(2,1)S(1)} %bitcast.52, pred[128,4]{1,0:T(8,128)(4,1)S(1)} %iota_compare_fusion.2, f32[16384]{0:T(1024)S(1)} %bitcast.53, pred[]{:T(512)S(6)} %and.50), kind=kOutput, calls=%fused_computation.6.clone.1 | convolution fusion | flops 135266304 | bytes 18416128 | tf_op jit(solution)/shard_map/while/body/eval_jaxpr/irkb,rkba->ira/dot_general | solution.py:48
  208.4 6.4 %collective-permute-done.1 = bf16[8,16384]{1,0:T(8,128)(2,1)S(1)} collective-permute-done((bf16[8,16384]{1,0:T(8,128)(2,1)S(1)}, bf16[8,16384]{1,0:T(8,128)(2,1)S(1)}, u32[]{:S(2)}, u32[]{:S(2)}) %collective-permute-start.1) | collective-permute-done | bytes 262176 | tf_op jit(solution)/shard_map/while/body/eval_jaxpr/ppermute | solution.py:14
  216.7 7.2 %fusion.22 = bf16[8,16384]{1,0:T(8,128)(2,1)S(1)} fusion(bf16[8,16384]{1,0:T(8,128)(2,1)S(1)} %get-tuple-element.269, bf16[128,4,128,128]{3,2,1,0:T(8,128)(2,1)} %get-tuple-element.283, bf16[128,4,8,128]{3,2,1,0:T(8,128)(2,1)S(1)} %bitcast.52, pred[128,4]{1,0:T(8,128)(4,1)S(1)} %iota_compare_fusion.2, f32[16384]{0:T(1024)S(1)} %bitcast.53, pred[]{:T(512)S(6)} %and.50), kind=kOutput, calls=%fused_computation.6.clone.1 | convolution fusion | flops 135266304 | bytes 18416128 | tf_op jit(solution)/shard_map/while/body/eval_jaxpr/irkb,rkba->ira/dot_general | solution.py:48
  237.2 6.8 %collective-permute-done.1 = bf16[8,16384]{1,0:T(8,128)(2,1)S(1)} collective-permute-done((bf16[8,16384]{1,0:T(8,128)(2,1)S(1)}, bf16[8,16384]{1,0:T(8,128)(2,1)S(1)}, u32[]{:S(2)}, u32[]{:S(2)}) %collective-permute-start.1) | collective-permute-done | bytes 262176 | tf_op jit(solution)/shard_map/while/body/eval_jaxpr/ppermute | solution.py:14
  245.9 7.2 %fusion.22 = bf16[8,16384]{1,0:T(8,128)(2,1)S(1)} fusion(bf16[8,16384]{1,0:T(8,128)(2,1)S(1)} %get-tuple-element.269, bf16[128,4,128,128]{3,2,1,0:T(8,128)(2,1)} %get-tuple-element.283, bf16[128,4,8,128]{3,2,1,0:T(8,128)(2,1)S(1)} %bitcast.52, pred[128,4]{1,0:T(8,128)(4,1)S(1)} %iota_compare_fusion.2, f32[16384]{0:T(1024)S(1)} %bitcast.53, pred[]{:T(512)S(6)} %and.50), kind=kOutput, calls=%fused_computation.6.clone.1 | convolution fusion | flops 135266304 | bytes 18416128 | tf_op jit(solution)/shard_map/while/body/eval_jaxpr/irkb,rkba->ira/dot_general | solution.py:48
  264.1 6.4 %collective-permute-done.1 = bf16[8,16384]{1,0:T(8,128)(2,1)S(1)} collective-permute-done((bf16[8,16384]{1,0:T(8,128)(2,1)S(1)}, bf16[8,16384]{1,0:T(8,128)(2,1)S(1)}, u32[]{:S(2)}, u32[]{:S(2)}) %collective-permute-start.1) | collective-permute-done | bytes 262176 | tf_op jit(solution)/shard_map/while/body/eval_jaxpr/ppermute | solution.py:14
  272.4 7.2 %fusion.22 = bf16[8,16384]{1,0:T(8,128)(2,1)S(1)} fusion(bf16[8,16384]{1,0:T(8,128)(2,1)S(1)} %get-tuple-element.269, bf16[128,4,128,128]{3,2,1,0:T(8,128)(2,1)} %get-tuple-element.283, bf16[128,4,8,128]{3,2,1,0:T(8,128)(2,1)S(1)} %bitcast.52, pred[128,4]{1,0:T(8,128)(4,1)S(1)} %iota_compare_fusion.2, f32[16384]{0:T(1024)S(1)} %bitcast.53, pred[]{:T(512)S(6)} %and.50), kind=kOutput, calls=%fused_computation.6.clone.1 | convolution fusion | flops 135266304 | bytes 18416128 | tf_op jit(solution)/shard_map/while/body/eval_jaxpr/irkb,rkba->ira/dot_general | solution.py:48
  293.5 6.5 %collective-permute-done.1 = bf16[8,16384]{1,0:T(8,128)(2,1)S(1)} collective-permute-done((bf16[8,16384]{1,0:T(8,128)(2,1)S(1)}, bf16[8,16384]{1,0:T(8,128)(2,1)S(1)}, u32[]{:S(2)}, u32[]{:S(2)}) %collective-permute-start.1) | collective-permute-done | bytes 262176 | tf_op jit(solution)/shard_map/while/body/eval_jaxpr/ppermute | solution.py:14
  301.8 7.2 %fusion.22 = bf16[8,16384]{1,0:T(8,128)(2,1)S(1)} fusion(bf16[8,16384]{1,0:T(8,128)(2,1)S(1)} %get-tuple-element.269, bf16[128,4,128,128]{3,2,1,0:T(8,128)(2,1)} %get-tuple-element.283, bf16[128,4,8,128]{3,2,1,0:T(8,128)(2,1)S(1)} %bitcast.52, pred[128,4]{1,0:T(8,128)(4,1)S(1)} %iota_compare_fusion.2, f32[16384]{0:T(1024)S(1)} %bitcast.53, pred[]{:T(512)S(6)} %and.50), kind=kOutput, calls=%fused_computation.6.clone.1 | convolution fusion | flops 135266304 | bytes 18416128 | tf_op jit(solution)/shard_map/while/body/eval_jaxpr/irkb,rkba->ira/dot_general | solution.py:48
  322.3 6.8 %collective-permute-done.1 = bf16[8,16384]{1,0:T(8,128)(2,1)S(1)} collective-permute-done((bf16[8,16384]{1,0:T(8,128)(2,1)S(1)}, bf16[8,16384]{1,0:T(8,128)(2,1)S(1)}, u32[]{:S(2)}, u32[]{:S(2)}) %collective-permute-start.1) | collective-permute-done | bytes 262176 | tf_op jit(solution)/shard_map/while/body/eval_jaxpr/ppermute | solution.py:14
  331.0 7.2 %fusion.22 = bf16[8,16384]{1,0:T(8,128)(2,1)S(1)} fusion(bf16[8,16384]{1,0:T(8,128)(2,1)S(1)} %get-tuple-element.269, bf16[128,4,128,128]{3,2,1,0:T(8,128)(2,1)} %get-tuple-element.283, bf16[128,4,8,128]{3,2,1,0:T(8,128)(2,1)S(1)} %bitcast.52, pred[128,4]{1,0:T(8,128)(4,1)S(1)} %iota_compare_fusion.2, f32[16384]{0:T(1024)S(1)} %bitcast.53, pred[]{:T(512)S(6)} %and.50), kind=kOutput, calls=%fused_computation.6.clone.1 | convolution fusion | flops 135266304 | bytes 18416128 | tf_op jit(solution)/shard_map/while/body/eval_jaxpr/irkb,rkba->ira/dot_general | solution.py:48
  351.4 5.9 %collective-permute-done.1 = bf16[8,16384]{1,0:T(8,128)(2,1)S(1)} collective-permute-done((bf16[8,16384]{1,0:T(8,128)(2,1)S(1)}, bf16[8,16384]{1,0:T(8,128)(2,1)S(1)}, u32[]{:S(2)}, u32[]{:S(2)}) %collective-permute-start.1) | collective-permute-done | bytes 262176 | tf_op jit(solution)/shard_map/while/body/eval_jaxpr/ppermute | solution.py:14
  359.2 7.2 %fusion.22 = bf16[8,16384]{1,0:T(8,128)(2,1)S(1)} fusion(bf16[8,16384]{1,0:T(8,128)(2,1)S(1)} %get-tuple-element.269, bf16[128,4,128,128]{3,2,1,0:T(8,128)(2,1)} %get-tuple-element.283, bf16[128,4,8,128]{3,2,1,0:T(8,128)(2,1)S(1)} %bitcast.52, pred[128,4]{1,0:T(8,128)(4,1)S(1)} %iota_compare_fusion.2, f32[16384]{0:T(1024)S(1)} %bitcast.53, pred[]{:T(512)S(6)} %and.50), kind=kOutput, calls=%fused_computation.6.clone.1 | convolution fusion | flops 135266304 | bytes 18416128 | tf_op jit(solution)/shard_map/while/body/eval_jaxpr/irkb,rkba->ira/dot_general | solution.py:48
  385.6 7.2 %fusion.22 = bf16[8,16384]{1,0:T(8,128)(2,1)S(1)} fusion(bf16[8,16384]{1,0:T(8,128)(2,1)S(1)} %get-tuple-element.269, bf16[128,4,128,128]{3,2,1,0:T(8,128)(2,1)} %get-tuple-element.283, bf16[128,4,8,128]{3,2,1,0:T(8,128)(2,1)S(1)} %bitcast.52, pred[128,4]{1,0:T(8,128)(4,1)S(1)} %iota_compare_fusion.2, f32[16384]{0:T(1024)S(1)} %bitcast.53, pred[]{:T(512)S(6)} %and.50), kind=kOutput, calls=%fused_computation.6.clone.1 | convolution fusion | flops 135266304 | bytes 18416128 | tf_op jit(solution)/shard_map/while/body/eval_jaxpr/irkb,rkba->ira/dot_general | solution.py:48
  407.4 6.7 %collective-permute-done.1 = bf16[8,16384]{1,0:T(8,128)(2,1)S(1)} collective-permute-done((bf16[8,16384]{1,0:T(8,128)(2,1)S(1)}, bf16[8,16384]{1,0:T(8,128)(2,1)S(1)}, u32[]{:S(2)}, u32[]{:S(2)}) %collective-permute-start.1) | collective-permute-done | bytes 262176 | tf_op jit(solution)/shard_map/while/body/eval_jaxpr/ppermute | solution.py:14
  416.0 7.2 %fusion.22 = bf16[8,16384]{1,0:T(8,128)(2,1)S(1)} fusion(bf16[8,16384]{1,0:T(8,128)(2,1)S(1)} %get-tuple-element.269, bf16[128,4,128,128]{3,2,1,0:T(8,128)(2,1)} %get-tuple-element.283, bf16[128,4,8,128]{3,2,1,0:T(8,128)(2,1)S(1)} %bitcast.52, pred[128,4]{1,0:T(8,128)(4,1)S(1)} %iota_compare_fusion.2, f32[16384]{0:T(1024)S(1)} %bitcast.53, pred[]{:T(512)S(6)} %and.50), kind=kOutput, calls=%fused_computation.6.clone.1 | convolution fusion | flops 135266304 | bytes 18416128 | tf_op jit(solution)/shard_map/while/body/eval_jaxpr/irkb,rkba->ira/dot_general | solution.py:48
  436.5 5.9 %collective-permute-done.1 = bf16[8,16384]{1,0:T(8,128)(2,1)S(1)} collective-permute-done((bf16[8,16384]{1,0:T(8,128)(2,1)S(1)}, bf16[8,16384]{1,0:T(8,128)(2,1)S(1)}, u32[]{:S(2)}, u32[]{:S(2)}) %collective-permute-start.1) | collective-permute-done | bytes 262176 | tf_op jit(solution)/shard_map/while/body/eval_jaxpr/ppermute | solution.py:14
  444.3 7.2 %fusion.22 = bf16[8,16384]{1,0:T(8,128)(2,1)S(1)} fusion(bf16[8,16384]{1,0:T(8,128)(2,1)S(1)} %get-tuple-element.269, bf16[128,4,128,128]{3,2,1,0:T(8,128)(2,1)} %get-tuple-element.283, bf16[128,4,8,128]{3,2,1,0:T(8,128)(2,1)S(1)} %bitcast.52, pred[128,4]{1,0:T(8,128)(4,1)S(1)} %iota_compare_fusion.2, f32[16384]{0:T(1024)S(1)} %bitcast.53, pred[]{:T(512)S(6)} %and.50), kind=kOutput, calls=%fused_computation.6.clone.1 | convolution fusion | flops 135266304 | bytes 18416128 | tf_op jit(solution)/shard_map/while/body/eval_jaxpr/irkb,rkba->ira/dot_general | solution.py:48
  (214 shorter events, 245.3 us)
Async XLA Ops:
  1.9 8.4 %collective-permute-start = (bf16[8,16384]{1,0:T(8,128)(2,1)S(1)}, bf16[8,16384]{1,0:T(8,128)(2,1)S(1)}, u32[]{:S(2)}, u32[]{:S(2)}) collective-permute-start(bf16[8,16384]{1,0:T(8,128)(2,1)S(1)} %get-tuple-element.269), channel_id=1, source_target_pairs={{1,0},{2,1},{3,2},{0,3},{5,4},{6,5},{7,6},{4,7},{9,8},{10,9},{11,1... | collective-permute-start | bytes 786440 | tf_op jit(solution)/shard_map/while/body/eval_jaxpr/ppermute | solution.py:15
  5.2 11.5 %collective-permute-start.1 = (bf16[8,16384]{1,0:T(8,128)(2,1)S(1)}, bf16[8,16384]{1,0:T(8,128)(2,1)S(1)}, u32[]{:S(2)}, u32[]{:S(2)}) collective-permute-start(bf16[8,16384]{1,0:T(8,128)(2,1)S(1)} %get-tuple-element.269), channel_id=1, source_target_pairs={{0,1},{1,2},{2,3},{3,0},{4,5},{5,6},{6,7},{7,4},{8,9},{9,10},{10,1... | collective-permute-start | bytes 786440 | tf_op jit(solution)/shard_map/while/body/eval_jaxpr/ppermute | solution.py:14
  32.3 10.1 %collective-permute-start.1 = (bf16[8,16384]{1,0:T(8,128)(2,1)S(1)}, bf16[8,16384]{1,0:T(8,128)(2,1)S(1)}, u32[]{:S(2)}, u32[]{:S(2)}) collective-permute-start(bf16[8,16384]{1,0:T(8,128)(2,1)S(1)} %get-tuple-element.269), channel_id=1, source_target_pairs={{0,1},{1,2},{2,3},{3,0},{4,5},{5,6},{6,7},{7,4},{8,9},{9,10},{10,1... | collective-permute-start | bytes 786440 | tf_op jit(solution)/shard_map/while/body/eval_jaxpr/ppermute | solution.py:14
  51.5 7.5 %collective-permute-start.2 = (bf16[8,16384]{1,0:T(8,128)(2,1)S(1)}, bf16[8,16384]{1,0:T(8,128)(2,1)S(1)}, u32[]{:S(2)}, u32[]{:S(2)}) collective-permute-start(bf16[8,16384]{1,0:T(8,128)(2,1)S(1)} %fusion.22), channel_id=1, source_target_pairs={{0,4},{4,8},{8,12},{12,16},{16,20},{20,24},{24,28},{28,0},{1,5},{5... | collective-permute-start | bytes 786440 | tf_op jit(solution)/shard_map/while/body/eval_jaxpr/ppermute | solution.py:22
  61.0 11.9 %collective-permute-start.1 = (bf16[8,16384]{1,0:T(8,128)(2,1)S(1)}, bf16[8,16384]{1,0:T(8,128)(2,1)S(1)}, u32[]{:S(2)}, u32[]{:S(2)}) collective-permute-start(bf16[8,16384]{1,0:T(8,128)(2,1)S(1)} %get-tuple-element.269), channel_id=1, source_target_pairs={{0,1},{1,2},{2,3},{3,0},{4,5},{5,6},{6,7},{7,4},{8,9},{9,10},{10,1... | collective-permute-start | bytes 786440 | tf_op jit(solution)/shard_map/while/body/eval_jaxpr/ppermute | solution.py:14
  81.9 6.8 %collective-permute-start.2 = (bf16[8,16384]{1,0:T(8,128)(2,1)S(1)}, bf16[8,16384]{1,0:T(8,128)(2,1)S(1)}, u32[]{:S(2)}, u32[]{:S(2)}) collective-permute-start(bf16[8,16384]{1,0:T(8,128)(2,1)S(1)} %fusion.22), channel_id=1, source_target_pairs={{0,4},{4,8},{8,12},{12,16},{16,20},{20,24},{24,28},{28,0},{1,5},{5... | collective-permute-start | bytes 786440 | tf_op jit(solution)/shard_map/while/body/eval_jaxpr/ppermute | solution.py:22
  88.7 6.4 %collective-permute-start = (bf16[8,16384]{1,0:T(8,128)(2,1)S(1)}, bf16[8,16384]{1,0:T(8,128)(2,1)S(1)}, u32[]{:S(2)}, u32[]{:S(2)}) collective-permute-start(bf16[8,16384]{1,0:T(8,128)(2,1)S(1)} %get-tuple-element.269), channel_id=1, source_target_pairs={{1,0},{2,1},{3,2},{0,3},{5,4},{6,5},{7,6},{4,7},{9,8},{10,9},{11,1... | collective-permute-start | bytes 786440 | tf_op jit(solution)/shard_map/while/body/eval_jaxpr/ppermute | solution.py:15
  90.2 10.9 %collective-permute-start.1 = (bf16[8,16384]{1,0:T(8,128)(2,1)S(1)}, bf16[8,16384]{1,0:T(8,128)(2,1)S(1)}, u32[]{:S(2)}, u32[]{:S(2)}) collective-permute-start(bf16[8,16384]{1,0:T(8,128)(2,1)S(1)} %get-tuple-element.269), channel_id=1, source_target_pairs={{0,1},{1,2},{2,3},{3,0},{4,5},{5,6},{6,7},{7,4},{8,9},{9,10},{10,1... | collective-permute-start | bytes 786440 | tf_op jit(solution)/shard_map/while/body/eval_jaxpr/ppermute | solution.py:14
  110.2 6.8 %collective-permute-start.2 = (bf16[8,16384]{1,0:T(8,128)(2,1)S(1)}, bf16[8,16384]{1,0:T(8,128)(2,1)S(1)}, u32[]{:S(2)}, u32[]{:S(2)}) collective-permute-start(bf16[8,16384]{1,0:T(8,128)(2,1)S(1)} %fusion.22), channel_id=1, source_target_pairs={{0,4},{4,8},{8,12},{12,16},{16,20},{20,24},{24,28},{28,0},{1,5},{5... | collective-permute-start | bytes 786440 | tf_op jit(solution)/shard_map/while/body/eval_jaxpr/ppermute | solution.py:22
  116.9 6.4 %collective-permute-start = (bf16[8,16384]{1,0:T(8,128)(2,1)S(1)}, bf16[8,16384]{1,0:T(8,128)(2,1)S(1)}, u32[]{:S(2)}, u32[]{:S(2)}) collective-permute-start(bf16[8,16384]{1,0:T(8,128)(2,1)S(1)} %get-tuple-element.269), channel_id=1, source_target_pairs={{1,0},{2,1},{3,2},{0,3},{5,4},{6,5},{7,6},{4,7},{9,8},{10,9},{11,1... | collective-permute-start | bytes 786440 | tf_op jit(solution)/shard_map/while/body/eval_jaxpr/ppermute | solution.py:15
  118.4 11.4 %collective-permute-start.1 = (bf16[8,16384]{1,0:T(8,128)(2,1)S(1)}, bf16[8,16384]{1,0:T(8,128)(2,1)S(1)}, u32[]{:S(2)}, u32[]{:S(2)}) collective-permute-start(bf16[8,16384]{1,0:T(8,128)(2,1)S(1)} %get-tuple-element.269), channel_id=1, source_target_pairs={{0,1},{1,2},{2,3},{3,0},{4,5},{5,6},{6,7},{7,4},{8,9},{9,10},{10,1... | collective-permute-start | bytes 786440 | tf_op jit(solution)/shard_map/while/body/eval_jaxpr/ppermute | solution.py:14
  146.1 10.6 %collective-permute-start.1 = (bf16[8,16384]{1,0:T(8,128)(2,1)S(1)}, bf16[8,16384]{1,0:T(8,128)(2,1)S(1)}, u32[]{:S(2)}, u32[]{:S(2)}) collective-permute-start(bf16[8,16384]{1,0:T(8,128)(2,1)S(1)} %get-tuple-element.269), channel_id=1, source_target_pairs={{0,1},{1,2},{2,3},{3,0},{4,5},{5,6},{6,7},{7,4},{8,9},{9,10},{10,1... | collective-permute-start | bytes 786440 | tf_op jit(solution)/shard_map/while/body/eval_jaxpr/ppermute | solution.py:14
  165.7 8.1 %collective-permute-start.2 = (bf16[8,16384]{1,0:T(8,128)(2,1)S(1)}, bf16[8,16384]{1,0:T(8,128)(2,1)S(1)}, u32[]{:S(2)}, u32[]{:S(2)}) collective-permute-start(bf16[8,16384]{1,0:T(8,128)(2,1)S(1)} %fusion.22), channel_id=1, source_target_pairs={{0,4},{4,8},{8,12},{12,16},{16,20},{20,24},{24,28},{28,0},{1,5},{5... | collective-permute-start | bytes 786440 | tf_op jit(solution)/shard_map/while/body/eval_jaxpr/ppermute | solution.py:22
  175.3 10.8 %collective-permute-start.1 = (bf16[8,16384]{1,0:T(8,128)(2,1)S(1)}, bf16[8,16384]{1,0:T(8,128)(2,1)S(1)}, u32[]{:S(2)}, u32[]{:S(2)}) collective-permute-start(bf16[8,16384]{1,0:T(8,128)(2,1)S(1)} %get-tuple-element.269), channel_id=1, source_target_pairs={{0,1},{1,2},{2,3},{3,0},{4,5},{5,6},{6,7},{7,4},{8,9},{9,10},{10,1... | collective-permute-start | bytes 786440 | tf_op jit(solution)/shard_map/while/body/eval_jaxpr/ppermute | solution.py:14
  195.2 6.8 %collective-permute-start.2 = (bf16[8,16384]{1,0:T(8,128)(2,1)S(1)}, bf16[8,16384]{1,0:T(8,128)(2,1)S(1)}, u32[]{:S(2)}, u32[]{:S(2)}) collective-permute-start(bf16[8,16384]{1,0:T(8,128)(2,1)S(1)} %fusion.22), channel_id=1, source_target_pairs={{0,4},{4,8},{8,12},{12,16},{16,20},{20,24},{24,28},{28,0},{1,5},{5... | collective-permute-start | bytes 786440 | tf_op jit(solution)/shard_map/while/body/eval_jaxpr/ppermute | solution.py:22
  203.5 11.4 %collective-permute-start.1 = (bf16[8,16384]{1,0:T(8,128)(2,1)S(1)}, bf16[8,16384]{1,0:T(8,128)(2,1)S(1)}, u32[]{:S(2)}, u32[]{:S(2)}) collective-permute-start(bf16[8,16384]{1,0:T(8,128)(2,1)S(1)} %get-tuple-element.269), channel_id=1, source_target_pairs={{0,1},{1,2},{2,3},{3,0},{4,5},{5,6},{6,7},{7,4},{8,9},{9,10},{10,1... | collective-permute-start | bytes 786440 | tf_op jit(solution)/shard_map/while/body/eval_jaxpr/ppermute | solution.py:14
  224.0 6.8 %collective-permute-start.2 = (bf16[8,16384]{1,0:T(8,128)(2,1)S(1)}, bf16[8,16384]{1,0:T(8,128)(2,1)S(1)}, u32[]{:S(2)}, u32[]{:S(2)}) collective-permute-start(bf16[8,16384]{1,0:T(8,128)(2,1)S(1)} %fusion.22), channel_id=1, source_target_pairs={{0,4},{4,8},{8,12},{12,16},{16,20},{20,24},{24,28},{28,0},{1,5},{5... | collective-permute-start | bytes 786440 | tf_op jit(solution)/shard_map/while/body/eval_jaxpr/ppermute | solution.py:22
  232.2 11.9 %collective-permute-start.1 = (bf16[8,16384]{1,0:T(8,128)(2,1)S(1)}, bf16[8,16384]{1,0:T(8,128)(2,1)S(1)}, u32[]{:S(2)}, u32[]{:S(2)}) collective-permute-start(bf16[8,16384]{1,0:T(8,128)(2,1)S(1)} %get-tuple-element.269), channel_id=1, source_target_pairs={{0,1},{1,2},{2,3},{3,0},{4,5},{5,6},{6,7},{7,4},{8,9},{9,10},{10,1... | collective-permute-start | bytes 786440 | tf_op jit(solution)/shard_map/while/body/eval_jaxpr/ppermute | solution.py:14
  260.4 10.1 %collective-permute-start.1 = (bf16[8,16384]{1,0:T(8,128)(2,1)S(1)}, bf16[8,16384]{1,0:T(8,128)(2,1)S(1)}, u32[]{:S(2)}, u32[]{:S(2)}) collective-permute-start(bf16[8,16384]{1,0:T(8,128)(2,1)S(1)} %get-tuple-element.269), channel_id=1, source_target_pairs={{0,1},{1,2},{2,3},{3,0},{4,5},{5,6},{6,7},{7,4},{8,9},{9,10},{10,1... | collective-permute-start | bytes 786440 | tf_op jit(solution)/shard_map/while/body/eval_jaxpr/ppermute | solution.py:14
  279.6 7.5 %collective-permute-start.2 = (bf16[8,16384]{1,0:T(8,128)(2,1)S(1)}, bf16[8,16384]{1,0:T(8,128)(2,1)S(1)}, u32[]{:S(2)}, u32[]{:S(2)}) collective-permute-start(bf16[8,16384]{1,0:T(8,128)(2,1)S(1)} %fusion.22), channel_id=1, source_target_pairs={{0,4},{4,8},{8,12},{12,16},{16,20},{20,24},{24,28},{28,0},{1,5},{5... | collective-permute-start | bytes 786440 | tf_op jit(solution)/shard_map/while/body/eval_jaxpr/ppermute | solution.py:22
  288.6 11.4 %collective-permute-start.1 = (bf16[8,16384]{1,0:T(8,128)(2,1)S(1)}, bf16[8,16384]{1,0:T(8,128)(2,1)S(1)}, u32[]{:S(2)}, u32[]{:S(2)}) collective-permute-start(bf16[8,16384]{1,0:T(8,128)(2,1)S(1)} %get-tuple-element.269), channel_id=1, source_target_pairs={{0,1},{1,2},{2,3},{3,0},{4,5},{5,6},{6,7},{7,4},{8,9},{9,10},{10,1... | collective-permute-start | bytes 786440 | tf_op jit(solution)/shard_map/while/body/eval_jaxpr/ppermute | solution.py:14
  309.0 6.8 %collective-permute-start.2 = (bf16[8,16384]{1,0:T(8,128)(2,1)S(1)}, bf16[8,16384]{1,0:T(8,128)(2,1)S(1)}, u32[]{:S(2)}, u32[]{:S(2)}) collective-permute-start(bf16[8,16384]{1,0:T(8,128)(2,1)S(1)} %fusion.22), channel_id=1, source_target_pairs={{0,4},{4,8},{8,12},{12,16},{16,20},{20,24},{24,28},{28,0},{1,5},{5... | collective-permute-start | bytes 786440 | tf_op jit(solution)/shard_map/while/body/eval_jaxpr/ppermute | solution.py:22
  317.2 11.9 %collective-permute-start.1 = (bf16[8,16384]{1,0:T(8,128)(2,1)S(1)}, bf16[8,16384]{1,0:T(8,128)(2,1)S(1)}, u32[]{:S(2)}, u32[]{:S(2)}) collective-permute-start(bf16[8,16384]{1,0:T(8,128)(2,1)S(1)} %get-tuple-element.269), channel_id=1, source_target_pairs={{0,1},{1,2},{2,3},{3,0},{4,5},{5,6},{6,7},{7,4},{8,9},{9,10},{10,1... | collective-permute-start | bytes 786440 | tf_op jit(solution)/shard_map/while/body/eval_jaxpr/ppermute | solution.py:14
  338.2 6.8 %collective-permute-start.2 = (bf16[8,16384]{1,0:T(8,128)(2,1)S(1)}, bf16[8,16384]{1,0:T(8,128)(2,1)S(1)}, u32[]{:S(2)}, u32[]{:S(2)}) collective-permute-start(bf16[8,16384]{1,0:T(8,128)(2,1)S(1)} %fusion.22), channel_id=1, source_target_pairs={{0,4},{4,8},{8,12},{12,16},{16,20},{20,24},{24,28},{28,0},{1,5},{5... | collective-permute-start | bytes 786440 | tf_op jit(solution)/shard_map/while/body/eval_jaxpr/ppermute | solution.py:22
  346.4 10.9 %collective-permute-start.1 = (bf16[8,16384]{1,0:T(8,128)(2,1)S(1)}, bf16[8,16384]{1,0:T(8,128)(2,1)S(1)}, u32[]{:S(2)}, u32[]{:S(2)}) collective-permute-start(bf16[8,16384]{1,0:T(8,128)(2,1)S(1)} %get-tuple-element.269), channel_id=1, source_target_pairs={{0,1},{1,2},{2,3},{3,0},{4,5},{5,6},{6,7},{7,4},{8,9},{9,10},{10,1... | collective-permute-start | bytes 786440 | tf_op jit(solution)/shard_map/while/body/eval_jaxpr/ppermute | solution.py:14
  373.7 10.0 %collective-permute-start.1 = (bf16[8,16384]{1,0:T(8,128)(2,1)S(1)}, bf16[8,16384]{1,0:T(8,128)(2,1)S(1)}, u32[]{:S(2)}, u32[]{:S(2)}) collective-permute-start(bf16[8,16384]{1,0:T(8,128)(2,1)S(1)} %get-tuple-element.269), channel_id=1, source_target_pairs={{0,1},{1,2},{2,3},{3,0},{4,5},{5,6},{6,7},{7,4},{8,9},{9,10},{10,1... | collective-permute-start | bytes 786440 | tf_op jit(solution)/shard_map/while/body/eval_jaxpr/ppermute | solution.py:14
  392.8 8.2 %collective-permute-start.2 = (bf16[8,16384]{1,0:T(8,128)(2,1)S(1)}, bf16[8,16384]{1,0:T(8,128)(2,1)S(1)}, u32[]{:S(2)}, u32[]{:S(2)}) collective-permute-start(bf16[8,16384]{1,0:T(8,128)(2,1)S(1)} %fusion.22), channel_id=1, source_target_pairs={{0,4},{4,8},{8,12},{12,16},{16,20},{20,24},{24,28},{28,0},{1,5},{5... | collective-permute-start | bytes 786440 | tf_op jit(solution)/shard_map/while/body/eval_jaxpr/ppermute | solution.py:22
  401.0 6.5 %collective-permute-start = (bf16[8,16384]{1,0:T(8,128)(2,1)S(1)}, bf16[8,16384]{1,0:T(8,128)(2,1)S(1)}, u32[]{:S(2)}, u32[]{:S(2)}) collective-permute-start(bf16[8,16384]{1,0:T(8,128)(2,1)S(1)} %get-tuple-element.269), channel_id=1, source_target_pairs={{1,0},{2,1},{3,2},{0,3},{5,4},{6,5},{7,6},{4,7},{9,8},{10,9},{11,1... | collective-permute-start | bytes 786440 | tf_op jit(solution)/shard_map/while/body/eval_jaxpr/ppermute | solution.py:15
  402.3 11.8 %collective-permute-start.1 = (bf16[8,16384]{1,0:T(8,128)(2,1)S(1)}, bf16[8,16384]{1,0:T(8,128)(2,1)S(1)}, u32[]{:S(2)}, u32[]{:S(2)}) collective-permute-start(bf16[8,16384]{1,0:T(8,128)(2,1)S(1)} %get-tuple-element.269), channel_id=1, source_target_pairs={{0,1},{1,2},{2,3},{3,0},{4,5},{5,6},{6,7},{7,4},{8,9},{9,10},{10,1... | collective-permute-start | bytes 786440 | tf_op jit(solution)/shard_map/while/body/eval_jaxpr/ppermute | solution.py:14
  423.2 6.8 %collective-permute-start.2 = (bf16[8,16384]{1,0:T(8,128)(2,1)S(1)}, bf16[8,16384]{1,0:T(8,128)(2,1)S(1)}, u32[]{:S(2)}, u32[]{:S(2)}) collective-permute-start(bf16[8,16384]{1,0:T(8,128)(2,1)S(1)} %fusion.22), channel_id=1, source_target_pairs={{0,4},{4,8},{8,12},{12,16},{16,20},{20,24},{24,28},{28,0},{1,5},{5... | collective-permute-start | bytes 786440 | tf_op jit(solution)/shard_map/while/body/eval_jaxpr/ppermute | solution.py:22
  431.5 10.9 %collective-permute-start.1 = (bf16[8,16384]{1,0:T(8,128)(2,1)S(1)}, bf16[8,16384]{1,0:T(8,128)(2,1)S(1)}, u32[]{:S(2)}, u32[]{:S(2)}) collective-permute-start(bf16[8,16384]{1,0:T(8,128)(2,1)S(1)} %get-tuple-element.269), channel_id=1, source_target_pairs={{0,1},{1,2},{2,3},{3,0},{4,5},{5,6},{6,7},{7,4},{8,9},{9,10},{10,1... | collective-permute-start | bytes 786440 | tf_op jit(solution)/shard_map/while/body/eval_jaxpr/ppermute | solution.py:14
  451.5 6.8 %collective-permute-start.2 = (bf16[8,16384]{1,0:T(8,128)(2,1)S(1)}, bf16[8,16384]{1,0:T(8,128)(2,1)S(1)}, u32[]{:S(2)}, u32[]{:S(2)}) collective-permute-start(bf16[8,16384]{1,0:T(8,128)(2,1)S(1)} %fusion.22), channel_id=1, source_target_pairs={{0,4},{4,8},{8,12},{12,16},{16,20},{20,24},{24,28},{28,0},{1,5},{5... | collective-permute-start | bytes 786440 | tf_op jit(solution)/shard_map/while/body/eval_jaxpr/ppermute | solution.py:22
  (32 other events, 287.0 us)
where the time goes:
time: 463 us; the launch traced here: 459 us
  waiting for transfers between devices  215 us (46%)
  matrix products  115 us (25%)
  starting transfers between devices  81.1 us (18%)
  local copies, waits for them, and re-layouts  33 us (7%)
  other arithmetic  13 us (3%)
    dot_general x16, matrix products, apply_layer(): jnp.einsum('irkb,rkba->ira', selected, weights, preferred_element_type=jn...  115 us
    ppermute x16, waiting for transfers between devices, extended_2(): before = lax.ppermute(last, axis, up)  103 us
    ppermute x16, waiting for transfers between devices, extended_2(): after = lax.ppermute(first, axis, down)  59.4 us
    ppermute x16, starting transfers between devices, shifted(): lax.ppermute(value, axis, [(i, (i + by) % devices) for i in range(devices)])  55.2 us
    ppermute x16, waiting for transfers between devices, shifted(): lax.ppermute(value, axis, [(i, (i + by) % devices) for i in range(devices)])  53.1 us
    gather x16, local copies, waits for them, and re-layouts, apply_layer(): selected = column_blocks[:, located, :]  28.8 us
    ppermute x16, starting transfers between devices, extended_2(): after = lax.ppermute(first, axis, down)  25.3 us
    lt x16, other arithmetic, shards(): jnp.arange(slots, dtype=jnp.int32)[None, :] < tile_counts[0][:, None]  11.8 us
  transfers between devices with their start and end apart: 48, of which 48 were waited for; matrix products, arithmetic and copies ran while one was open for 3% of the time, Pallas kernels for 0%

commit v1 on v0

v1 whole, which is shorter than its diff:
```python
import functools

import jax
import jax.numpy as jnp
from jax import lax
from jax.experimental import pallas as pl
from jax.experimental.pallas import tpu as pltpu
from jax.sharding import PartitionSpec as P

MESH = pl.DeviceIdType.MESH


def kernel(S, B, R, K, T, UNROLL, idx_ref, bias_ref, images_ref, w_hbm, out_ref, w, homes, landed, snd, *rest):
    exts, (w_sem, home_sem, send_sem, recv_sem, out_sem) = rest[:S], rest[S:]
    s = lax.axis_index("section")
    b = lax.axis_index("blk")
    right, left = lax.rem(b + 1, B), lax.rem(b + B - 1, B)
    H = R // 2
    parts = w_sem.shape[0]
    rows_part = R // parts

    def load(p):
        rows = pl.ds(p * rows_part, rows_part)
        return pltpu.make_async_copy(w_hbm.at[0, rows], w.at[rows], w_sem.at[p])

    for p in range(parts):
        load(p).start()

    barrier = pltpu.get_barrier_semaphore()

    def greet(d, carry):
        to = lax.rem(s + d, S)
        for place in (left, right):
            pl.semaphore_signal(barrier, inc=1, device_id=(to, place), device_id_type=MESH)

        @pl.when(d > 0)
        def _():
            pl.semaphore_signal(barrier, inc=1, device_id=(to, b), device_id_type=MESH)

        return carry

    lax.fori_loop(0, S, greet, 0)

    for ext in exts:
        ext[4 * H] = jnp.zeros(ext.shape[1:], ext.dtype)

    def packed(r, carry):
        homes[r] = images_ref[:, pl.ds(pl.multiple_of(r * T, T), T)]
        return carry

    lax.fori_loop(0, R, packed, 0, unroll=UNROLL)

    pl.semaphore_wait(barrier, 3 * S - 1)

    low, high = pl.ds(0, H), pl.ds(H, H)

    def hops(src, g, to, sem, which):
        half = low if which == 0 else high
        own = exts[g].at[pl.ds(H, H)] if which == 0 else exts[g].at[pl.ds(2 * H, H)]
        halo = exts[g].at[pl.ds(3 * H, H)] if which == 0 else exts[g].at[pl.ds(0, H)]
        place = left if which == 0 else right
        mine = pltpu.make_async_remote_copy(
            src_ref=src.at[half], dst_ref=own, send_sem=sem.at[2 * which], recv_sem=recv_sem.at[g, 2 * which],
            device_id=(to, b), device_id_type=MESH)
        beside = pltpu.make_async_remote_copy(
            src_ref=src.at[half], dst_ref=halo, send_sem=sem.at[2 * which + 1],
            recv_sem=recv_sem.at[g, 2 * which + 1], device_id=(to, place), device_id_type=MESH)
        return mine, beside

    def local(g, which):
        half = low if which == 0 else high
        return pltpu.make_async_copy(
            homes.at[half], exts[g].at[pl.ds((1 + which) * H, H)], recv_sem.at[g, 2 * which])

    for g in range(S):
        @pl.when(s == g)
        def _(g=g):
            for which in (0, 1):
                mine, beside = hops(homes, g, 0, home_sem, which)
                if g == 0:
                    local(g, which).start()
                else:
                    mine.start()
                beside.start()

    def deliver(g, which):
        half = low if which == 0 else high
        return pltpu.make_async_remote_copy(
            src_ref=snd.at[g, half], dst_ref=landed.at[half], send_sem=send_sem.at[g, 2 * which],
            recv_sem=out_sem.at[which], device_id=(g, b), device_id_type=MESH)

    def keep(g, which):
        half = low if which == 0 else high
        return pltpu.make_async_copy(snd.at[g, half], landed.at[half], out_sem.at[which])

    def compute(g, first, count):
        ext = exts[g]

        def row(r, carry):
            x = jnp.concatenate(
                [ext[idx_ref[r * K + k]] for k in range(K)], axis=1)
            y = jnp.dot(x, w[r].reshape(K * T, T), preferred_element_type=jnp.float32)
            at = pl.ds(pl.multiple_of(r * T, T), T)
            y = jnp.minimum(jnp.maximum(y + bias_ref[:, at], 0.0), 32.0)
            snd[g, r] = y.astype(snd.dtype)
            return carry

        lax.fori_loop(first, first + count, row, 0, unroll=UNROLL)

    for g in range(S):
        for which in (0, 1):
            for copy in hops(snd.at[g], g, 0, send_sem.at[g], which):
                copy.wait_recv()
        for which in (0, 1):
            first = which * (R // 2)
            if g == 0:
                for p in range(which * parts // 2, (which + 1) * parts // 2):
                    load(p).wait()
                    compute(g, p * rows_part, rows_part)
            else:
                compute(g, first, R // 2)

            @pl.when(s < S - 1)
            def _(g=g, which=which):
                for copy in hops(snd.at[g], g, s + 1, send_sem.at[g], which):
                    copy.start()

            @pl.when(s == S - 1)
            def _(g=g, which=which):
                if g == S - 1:
                    keep(g, which).start()
                else:
                    deliver(g, which).start()

    for which in (0, 1):
        mine, beside = hops(homes, 0, 0, home_sem, which)
        beside.wait_send()

        @pl.when(s > 0)
        def _(mine=mine):
            mine.wait_send()

        deliver(0, which).wait_recv()

    def unpacked(r, carry):
        out_ref[:, pl.ds(pl.multiple_of(r * T, T), T)] = landed[r]
        return carry

    lax.fori_loop(0, R, unpacked, 0, unroll=UNROLL)
    for g in range(S):
        for which in (0, 1):
            @pl.when(s < S - 1)
            def _(g=g, which=which):
                for copy in hops(snd.at[g], g, 0, send_sem.at[g], which):
                    copy.wait_send()

            if g < S - 1:
                @pl.when(s == S - 1)
                def _(g=g, which=which):
                    deliver(g, which).wait_send()


def shards(S, B, images, tile_weights, tile_columns, tile_counts, bias):
    rows, width = images.shape
    _, R, K, T, _ = tile_weights.shape
    first = lax.axis_index("blk") * R
    place = (tile_columns[0] - first + R // 2) % (R * B)
    live = jnp.arange(K, dtype=jnp.int32)[None, :] < tile_counts[0][:, None]
    idx = jnp.where(live, place, 2 * R).reshape(R * K)
    parts = 8
    vmem = pl.BlockSpec(memory_space=pltpu.VMEM)
    return pl.pallas_call(
        functools.partial(kernel, S, B, R, K, T, min(4, R // parts)),
        out_shape=jax.ShapeDtypeStruct((rows, width), images.dtype),
        in_specs=[pl.BlockSpec(memory_space=pltpu.SMEM), vmem, vmem, pl.BlockSpec(memory_space=pl.ANY)],
        out_specs=vmem,
        scratch_shapes=[
            pltpu.VMEM((R, K, T, T), tile_weights.dtype),
            pltpu.VMEM((R, rows, T), images.dtype),
            pltpu.VMEM((R, rows, T), images.dtype),
            pltpu.VMEM((S, R, rows, T), images.dtype),
            *[pltpu.VMEM((2 * R + 1, rows, T), images.dtype) for _ in range(S)],
            pltpu.SemaphoreType.DMA((parts,)),
            pltpu.SemaphoreType.DMA((4,)),
            pltpu.SemaphoreType.DMA((S, 4)),
            pltpu.SemaphoreType.DMA((S, 4)),
            pltpu.SemaphoreType.DMA((2,)),
        ],
        compiler_params=pltpu.CompilerParams(
            collective_id=0, has_side_effects=True, vmem_limit_bytes=52 * 2**20),
    )(idx, bias, images, tile_weights)


def solution(mesh):
    placed = (
        P("section", "blk"),
        P("section", "blk", None, None, None),
        P("section", "blk", None),
        P("section", "blk"),
        P("section", "blk"),
    )
    return jax.shard_map(
        functools.partial(shards, mesh.shape["section"], mesh.shape["blk"]),
        mesh=mesh, in_specs=placed, out_specs=P("section", "blk"), check_vma=False)
```

time: 463 us -> 151 us (0.33)
  waiting for transfers between devices: 215 us -> 0 us
  Pallas kernels: 0 us -> 147 us
  matrix products: 115 us -> 0 us
  starting transfers between devices: 81.1 us -> 0 us
  local copies, waits for them, and re-layouts: 33 us -> 2.82 us
  other arithmetic: 13 us -> 1.43 us
    ppermute x48 -> x0, waiting for transfers between devices: 215 us -> none  [the longest x16 103 us: extended_2(): before = lax.ppermute(last, axis, up)]
    pallas_call x0 -> x1, Pallas kernels: none -> 147 us  [shards(): pl.pallas_call(functools.partial(kernel, S, B, R, K, T, min(4, R // parts...]
    dot_general x16 -> x0, matrix products: 115 us -> none  [apply_layer(): jnp.einsum('irkb,rkba->ira', selected, weights, preferred_element_type=jn...]
    ppermute x48 -> x0, starting transfers between devices: 81.1 us -> none  [the longest x16 55.2 us: shifted(): lax.ppermute(value, axis, [(i, (i + by) % devices) for i in range(devices)])]
    gather x16 -> x0, local copies, waits for them, and re-layouts: 28.8 us -> none  [apply_layer(): selected = column_blocks[:, located, :]]
    lt x16 -> x1, other arithmetic: 11.8 us -> 0.74 us  [shards(): live = jnp.arange(K, dtype=jnp.int32)[None, :] < tile_counts[0][:, None]]
  transfers between devices with their start and end apart: 48 -> 0, of which waited for: 48 -> 0; matrix products, arithmetic and copies ran while one was open for 3% -> 0% of each run, Pallas kernels for 0% -> 0%
where the time goes in v1:
time: 151 us
  Pallas kernels  147 us (97%)
  local copies, waits for them, and re-layouts  2.82 us (2%)
    pallas_call x1, Pallas kernels, shards(): pl.pallas_call(functools.partial(kernel, S, B, R, K, T, min(4, R // parts...  147 us

profile of v1, /device:TPU:7, one launch (start us, length us, event | category | flops | bytes accessed | tf_op | source)
XLA Modules:
  0.0 150.9 jit_solution(4179592840596365026)
XLA Ops:
  0.0 0.7 subtract_add_fusion
  0.7 0.7 iota_compare_fusion
  1.4 0.1 lt.29
  1.5 0.1 copy.6
  1.7 0.1 add.19
  1.8 0.0 copy-start
  1.8 0.9 copy-done
  2.7 0.0 copy-start.1
  2.7 0.8 copy-done.1
  3.6 146.6 %shard_map.55 = bf16[8,16384]{1,0:T(8,128)(2,1)S(1)} custom-call(s32[512]{0:T(512)S(1)} %fusion.1.idx_ref, f32[1,16384]{1,0:T(1,128)S(1)} %copy-done.1, bf16[8,16384]{1,0:T(8,128)(2,1)S(1)} %copy-done, bf16[1,128,4,128,128]{4,3,2,1,0:T(8,128)(2,1)} %w_hbm.1), custom_call_target="tpu_custom_call" | custom-call | tf_op jit(solution)/shard_map/pallas_call | solution.py:172
  150.1 0.7 copy.8
  (1 shorter events, 0.0 us)
Async XLA Ops:
  1.8 1.0 copy-start
  2.7 0.8 copy-start.1

commit v2 on v1

v2 whole, which is shorter than its diff:
```python
import functools

import jax
import jax.numpy as jnp
from jax import lax
from jax.experimental import pallas as pl
from jax.experimental.pallas import tpu as pltpu
from jax.sharding import PartitionSpec as P

MESH = pl.DeviceIdType.MESH


def kernel(S, B, R, K, T, Q, UNROLL, idx_ref, bias_ref, images_ref, w_hbm, out_ref, w, homes, landed, snd, *rest):
    G = S * Q
    exts, (w_sem, home_sem, send_sem, recv_sem, out_sem) = rest[:G], rest[G:]
    s = lax.axis_index("section")
    b = lax.axis_index("blk")
    right, left = lax.rem(b + 1, B), lax.rem(b + B - 1, B)
    H = R // 2
    M = images_ref.shape[0] // Q
    parts = w_sem.shape[0]
    rows_part = R // parts

    def load(p):
        rows = pl.ds(p * rows_part, rows_part)
        return pltpu.make_async_copy(w_hbm.at[0, rows], w.at[rows], w_sem.at[p])

    for p in range(parts):
        load(p).start()

    barrier = pltpu.get_barrier_semaphore()

    def greet(d, carry):
        to = lax.rem(s + d, S)
        for place in (left, right):
            pl.semaphore_signal(barrier, inc=1, device_id=(to, place), device_id_type=MESH)

        @pl.when(d > 0)
        def _():
            pl.semaphore_signal(barrier, inc=1, device_id=(to, b), device_id_type=MESH)

        return carry

    lax.fori_loop(0, S, greet, 0)

    for ext in exts:
        ext[2 * R] = jnp.zeros(ext.shape[1:], ext.dtype)

    def packed(r, carry):
        block = images_ref[:, pl.ds(pl.multiple_of(r * T, T), T)]
        for q in range(Q):
            homes[q, r] = block[q * M:(q + 1) * M]
        return carry

    lax.fori_loop(0, R, packed, 0, unroll=4)
    pl.semaphore_wait(barrier, 3 * S - 1)

    def hops(src, g, to, sem, half):
        rows = src.at[pl.ds(half * H, H)]
        mine = pltpu.make_async_remote_copy(
            src_ref=rows, dst_ref=exts[g].at[pl.ds(H + half * H, H)], send_sem=sem.at[2 * half],
            recv_sem=recv_sem.at[g, 2 * half], device_id=(to, b), device_id_type=MESH)
        beside = pltpu.make_async_remote_copy(
            src_ref=rows, dst_ref=exts[g].at[pl.ds((1 - half) * 3 * H, H)], send_sem=sem.at[2 * half + 1],
            recv_sem=recv_sem.at[g, 2 * half + 1], device_id=(to, lax.rem(b + B - 1 + 2 * half, B)),
            device_id_type=MESH)
        return mine, beside

    def local(g, half):
        return pltpu.make_async_copy(
            homes.at[g, pl.ds(half * H, H)], exts[g].at[pl.ds(H + half * H, H)], recv_sem.at[g, 2 * half])

    for g in range(G):
        @pl.when(s == g // Q)
        def _(g=g):
            for half in (0, 1):
                mine, beside = hops(homes.at[g % Q], g, 0, home_sem.at[g % Q], half)
                if g < Q:
                    local(g, half).start()
                else:
                    mine.start()
                beside.start()

    def deliver(g, half):
        rows = pl.ds(half * H, H)
        return pltpu.make_async_remote_copy(
            src_ref=snd.at[g, rows], dst_ref=landed.at[g % Q, rows], send_sem=send_sem.at[g, 2 * half],
            recv_sem=out_sem.at[g % Q, half], device_id=(g // Q, b), device_id_type=MESH)

    def keep(g, half):
        rows = pl.ds(half * H, H)
        return pltpu.make_async_copy(snd.at[g, rows], landed.at[g % Q, rows], out_sem.at[g % Q, half])

    def stage(g):
        ext = exts[g]

        def row(r, carry):
            x = jnp.concatenate([ext[idx_ref[r * K + k]] for k in range(K)], axis=1)
            y = jnp.dot(x, w[r].reshape(K * T, T), preferred_element_type=jnp.float32)
            y = y + bias_ref[:, pl.ds(pl.multiple_of(r * T, T), T)]
            snd[g, r] = jnp.minimum(jnp.maximum(y, 0.0), 32.0).astype(snd.dtype)
            return carry

        def halves(half, carry):
            if g == 0:
                for p in range(parts // 2):
                    load(half * (parts // 2) + p).wait()
            lax.fori_loop(half * (H // UNROLL), (half + 1) * (H // UNROLL), rows, 0)

            @pl.when(s < S - 1)
            def _():
                for copy in hops(snd.at[g], g, s + 1, send_sem.at[g], half):
                    copy.start()

            @pl.when(s == S - 1)
            def _():
                (keep if g // Q == S - 1 else deliver)(g, half).start()

            return carry

        def rows(i, carry):
            for j in range(UNROLL):
                row(i * UNROLL + j, 0)
            return carry

        lax.fori_loop(0, 2, halves, 0)

    for g in range(G):
        for half in (0, 1):
            for copy in hops(snd.at[g], g, 0, send_sem.at[g], half):
                copy.wait_recv()
        stage(g)

    for q in range(Q):
        for half in (0, 1):
            mine, beside = hops(homes.at[q], q, 0, home_sem.at[q], half)
            beside.wait_send()

            @pl.when(s > 0)
            def _(mine=mine):
                mine.wait_send()

            deliver(q, half).wait_recv()

    def unpacked(r, carry):
        out_ref[:, pl.ds(pl.multiple_of(r * T, T), T)] = jnp.concatenate([landed[q, r] for q in range(Q)], axis=0)
        return carry

    lax.fori_loop(0, R, unpacked, 0, unroll=4)
    for g in range(G):
        for half in (0, 1):
            @pl.when(s < S - 1)
            def _(g=g, half=half):
                for copy in hops(snd.at[g], g, 0, send_sem.at[g], half):
                    copy.wait_send()

            if g // Q < S - 1:
                @pl.when(s == S - 1)
                def _(g=g, half=half):
                    deliver(g, half).wait_send()


def shards(S, B, images, tile_weights, tile_columns, tile_counts, bias):
    rows, width = images.shape
    _, R, K, T, _ = tile_weights.shape
    first = lax.axis_index("blk") * R
    place = (tile_columns[0] - first + R // 2) % (R * B)
    live = jnp.arange(K, dtype=jnp.int32)[None, :] < tile_counts[0][:, None]
    idx = jnp.where(live, place, 2 * R).reshape(R * K)
    parts = 8
    Q = 2 if rows % 8 == 0 else 1
    M, G = rows // Q, S * Q
    vmem = pl.BlockSpec(memory_space=pltpu.VMEM)
    return pl.pallas_call(
        functools.partial(kernel, S, B, R, K, T, Q, max(1, min(R // 2, 256 // S))),
        out_shape=jax.ShapeDtypeStruct((rows, width), images.dtype),
        in_specs=[pl.BlockSpec(memory_space=pltpu.SMEM), vmem, vmem, pl.BlockSpec(memory_space=pl.ANY)],
        out_specs=vmem,
        scratch_shapes=[
            pltpu.VMEM((R, K, T, T), tile_weights.dtype),
            pltpu.VMEM((Q, R, M, T), images.dtype),
            pltpu.VMEM((Q, R, M, T), images.dtype),
            pltpu.VMEM((G, R, M, T), images.dtype),
            *[pltpu.VMEM((2 * R + 1, M, T), images.dtype) for _ in range(G)],
            pltpu.SemaphoreType.DMA((parts,)),
            pltpu.SemaphoreType.DMA((Q, 4)),
            pltpu.SemaphoreType.DMA((G, 4)),
            pltpu.SemaphoreType.DMA((G, 4)),
            pltpu.SemaphoreType.DMA((Q, 2)),
        ],
        compiler_params=pltpu.CompilerParams(
            collective_id=0, has_side_effects=True, vmem_limit_bytes=52 * 2**20),
    )(idx, bias, images, tile_weights)


def solution(mesh):
    placed = (
        P("section", "blk"),
        P("section", "blk", None, None, None),
        P("section", "blk", None),
        P("section", "blk"),
        P("section", "blk"),
    )
    return jax.shard_map(
        functools.partial(shards, mesh.shape["section"], mesh.shape["blk"]),
        mesh=mesh, in_specs=placed, out_specs=P("section", "blk"), check_vma=False)
```

time: 151 us -> 112 us (0.74)
  Pallas kernels: 147 us -> 108 us
    pallas_call x1, Pallas kernels: 147 us -> 108 us  [shards(): pl.pallas_call(functools.partial(kernel, S, B, R, K, T, Q, max(1, min(R /...]
where the time goes in v2:
time: 112 us
  Pallas kernels  108 us (96%)
  local copies, waits for them, and re-layouts  2.82 us (3%)
  other arithmetic  1.43 us (1%)
    pallas_call x1, Pallas kernels, shards(): pl.pallas_call(functools.partial(kernel, S, B, R, K, T, Q, max(1, min(R /...  108 us
    unnamed x5, local copies, waits for them, and re-layouts  2.49 us

profile of v2, /device:TPU:7, one launch (start us, length us, event | category | flops | bytes accessed | tf_op | source)
XLA Modules:
  0.0 111.8 jit_solution(3665783138373954002)
XLA Ops:
  0.0 0.7 subtract_add_fusion
  0.7 0.7 iota_compare_fusion
  1.4 0.1 lt.29
  1.5 0.1 copy.6
  1.7 0.1 add.19
  1.8 0.0 copy-start
  1.8 0.9 copy-done
  2.7 0.0 copy-start.1
  2.7 0.8 copy-done.1
  3.6 107.6 %shard_map.55 = bf16[8,16384]{1,0:T(8,128)(2,1)S(1)} custom-call(s32[512]{0:T(512)S(1)} %fusion.1.idx_ref, f32[1,16384]{1,0:T(1,128)S(1)} %copy-done.1, bf16[8,16384]{1,0:T(8,128)(2,1)S(1)} %copy-done, bf16[1,128,4,128,128]{4,3,2,1,0:T(8,128)(2,1)} %w_hbm.1), custom_call_target="tpu_custom_call" | custom-call | tf_op jit(solution)/shard_map/pallas_call | solution.py:174
  111.1 0.7 copy.8
  (1 shorter events, 0.0 us)
Async XLA Ops:
  1.8 1.0 copy-start
  2.7 0.8 copy-start.1

commit v3 on v2

v3 whole, which is shorter than its diff:
```python
import functools

import jax
import jax.numpy as jnp
from jax import lax
from jax.experimental import pallas as pl
from jax.experimental.pallas import tpu as pltpu
from jax.sharding import PartitionSpec as P

MESH = pl.DeviceIdType.MESH


def kernel(S, B, R, K, T, Q, UNROLL, idx_ref, bias_ref, images_ref, w_hbm, out_ref, w, homes, landed, snd, *rest):
    G = S * Q
    exts, (w_sem, home_sem, send_sem, recv_sem, out_sem) = rest[:G], rest[G:]
    s = lax.axis_index("section")
    b = lax.axis_index("blk")
    right, left = lax.rem(b + 1, B), lax.rem(b + B - 1, B)
    H, C = R // 2, 4
    L = R // C
    M = images_ref.shape[0] // Q
    parts = w_sem.shape[0]
    rows_part = R // parts

    def load(p):
        rows = pl.ds(p * rows_part, rows_part)
        return pltpu.make_async_copy(w_hbm.at[0, rows], w.at[rows], w_sem.at[p])

    for p in range(parts):
        load(p).start()

    barrier = pltpu.get_barrier_semaphore()

    def greet(d, carry):
        to = lax.rem(s + d, S)
        for place in (left, right):
            pl.semaphore_signal(barrier, inc=1, device_id=(to, place), device_id_type=MESH)

        @pl.when(d > 0)
        def _():
            pl.semaphore_signal(barrier, inc=1, device_id=(to, b), device_id_type=MESH)

        return carry

    lax.fori_loop(0, S, greet, 0)

    for ext in exts:
        ext[2 * R] = jnp.zeros(ext.shape[1:], ext.dtype)

    def packed(r, carry):
        block = images_ref[:, pl.ds(pl.multiple_of(r * T, T), T)]
        for q in range(Q):
            homes[q, r] = block[q * M:(q + 1) * M]
        return carry

    lax.fori_loop(0, R, packed, 0, unroll=4)
    pl.semaphore_wait(barrier, 3 * S - 1)

    def hops(src, g, to, sem, part):
        rows = src.at[pl.ds(part * L, L)]
        mine = pltpu.make_async_remote_copy(
            src_ref=rows, dst_ref=exts[g].at[pl.ds(H + part * L, L)], send_sem=sem.at[2 * part],
            recv_sem=recv_sem.at[g, 2 * part], device_id=(to, b), device_id_type=MESH)
        beside = pltpu.make_async_remote_copy(
            src_ref=rows, dst_ref=exts[g].at[pl.ds((part * L + 3 * H) % (4 * H), L)], send_sem=sem.at[2 * part + 1],
            recv_sem=recv_sem.at[g, 2 * part + 1], device_id=(to, lax.rem(b + B - 1 + 2 * (part // (C // 2)), B)),
            device_id_type=MESH)
        return beside, mine

    def local(g, part):
        return pltpu.make_async_copy(
            homes.at[g, pl.ds(part * L, L)], exts[g].at[pl.ds(H + part * L, L)], recv_sem.at[g, 2 * part])

    for g in range(G):
        @pl.when(s == g // Q)
        def _(g=g):
            for part in range(C):
                beside, mine = hops(homes.at[g % Q], g, 0, home_sem.at[g % Q], part)
                beside.start()
                if g < Q:
                    local(g, part).start()
                else:
                    mine.start()

    def deliver(g, part):
        rows = pl.ds(part * L, L)
        return pltpu.make_async_remote_copy(
            src_ref=snd.at[g, rows], dst_ref=landed.at[g % Q, rows], send_sem=send_sem.at[g, 2 * part],
            recv_sem=out_sem.at[g % Q, part], device_id=(g // Q, b), device_id_type=MESH)

    def keep(g, part):
        rows = pl.ds(part * L, L)
        return pltpu.make_async_copy(snd.at[g, rows], landed.at[g % Q, rows], out_sem.at[g % Q, part])

    def stage(g):
        ext = exts[g]

        def row(r, carry):
            x = jnp.concatenate([ext[idx_ref[r * K + k]] for k in range(K)], axis=1)
            y = jnp.dot(x, w[r].reshape(K * T, T), preferred_element_type=jnp.float32)
            y = y + bias_ref[:, pl.ds(pl.multiple_of(r * T, T), T)]
            snd[g, r] = jnp.minimum(jnp.maximum(y, 0.0), 32.0).astype(snd.dtype)
            return carry

        def quarters(part, carry):
            if g == 0:
                for p in range(parts // C):
                    load(part * (parts // C) + p).wait()
            lax.fori_loop(part * (L // UNROLL), (part + 1) * (L // UNROLL), rows, 0)

            @pl.when(s < S - 1)
            def _():
                for copy in hops(snd.at[g], g, s + 1, send_sem.at[g], part):
                    copy.start()

            @pl.when(s == S - 1)
            def _():
                (keep if g // Q == S - 1 else deliver)(g, part).start()

            return carry

        def rows(i, carry):
            for j in range(UNROLL):
                row(i * UNROLL + j, 0)
            return carry

        lax.fori_loop(0, C, quarters, 0)

    for g in range(G):
        for part in range(C):
            for copy in hops(snd.at[g], g, 0, send_sem.at[g], part):
                copy.wait_recv()
        stage(g)

    for q in range(Q):
        for part in range(C):
            beside, mine = hops(homes.at[q], q, 0, home_sem.at[q], part)
            beside.wait_send()

            @pl.when(s > 0)
            def _(mine=mine):
                mine.wait_send()

            deliver(q, part).wait_recv()

    def unpacked(r, carry):
        out_ref[:, pl.ds(pl.multiple_of(r * T, T), T)] = jnp.concatenate([landed[q, r] for q in range(Q)], axis=0)
        return carry

    lax.fori_loop(0, R, unpacked, 0, unroll=4)
    for g in range(G):
        for part in range(C):
            @pl.when(s < S - 1)
            def _(g=g, part=part):
                for copy in hops(snd.at[g], g, 0, send_sem.at[g], part):
                    copy.wait_send()

            if g // Q < S - 1:
                @pl.when(s == S - 1)
                def _(g=g, part=part):
                    deliver(g, part).wait_send()


def shards(S, B, images, tile_weights, tile_columns, tile_counts, bias):
    rows, width = images.shape
    _, R, K, T, _ = tile_weights.shape
    first = lax.axis_index("blk") * R
    place = (tile_columns[0] - first + R // 2) % (R * B)
    live = jnp.arange(K, dtype=jnp.int32)[None, :] < tile_counts[0][:, None]
    idx = jnp.where(live, place, 2 * R).reshape(R * K)
    parts = 8
    Q = 2 if rows % 8 == 0 else 1
    M, G = rows // Q, S * Q
    vmem = pl.BlockSpec(memory_space=pltpu.VMEM)
    return pl.pallas_call(
        functools.partial(kernel, S, B, R, K, T, Q, max(1, min(R // 4, 256 // S))),
        out_shape=jax.ShapeDtypeStruct((rows, width), images.dtype),
        in_specs=[pl.BlockSpec(memory_space=pltpu.SMEM), vmem, vmem, pl.BlockSpec(memory_space=pl.ANY)],
        out_specs=vmem,
        scratch_shapes=[
            pltpu.VMEM((R, K, T, T), tile_weights.dtype),
            pltpu.VMEM((Q, R, M, T), images.dtype),
            pltpu.VMEM((Q, R, M, T), images.dtype),
            pltpu.VMEM((G, R, M, T), images.dtype),
            *[pltpu.VMEM((2 * R + 1, M, T), images.dtype) for _ in range(G)],
            pltpu.SemaphoreType.DMA((parts,)),
            pltpu.SemaphoreType.DMA((Q, 8)),
            pltpu.SemaphoreType.DMA((G, 8)),
            pltpu.SemaphoreType.DMA((G, 8)),
            pltpu.SemaphoreType.DMA((Q, 4)),
        ],
        compiler_params=pltpu.CompilerParams(
            collective_id=0, has_side_effects=True, vmem_limit_bytes=52 * 2**20),
    )(idx, bias, images, tile_weights)


def solution(mesh):
    placed = (
        P("section", "blk"),
        P("section", "blk", None, None, None),
        P("section", "blk", None),
        P("section", "blk"),
        P("section", "blk"),
    )
    return jax.shard_map(
        functools.partial(shards, mesh.shape["section"], mesh.shape["blk"]),
        mesh=mesh, in_specs=placed, out_specs=P("section", "blk"), check_vma=False)
```

time: 112 us -> 110 us (0.982)
  Pallas kernels: 108 us -> 106 us
    pallas_call x1, Pallas kernels: 108 us -> 106 us  [shards(): pl.pallas_call(functools.partial(kernel, S, B, R, K, T, Q, max(1, min(R /...]
where the time goes in v3:
time: 110 us
  Pallas kernels  106 us (96%)
  local copies, waits for them, and re-layouts  2.82 us (3%)
  other arithmetic  1.43 us (1%)
    pallas_call x1, Pallas kernels, shards(): pl.pallas_call(functools.partial(kernel, S, B, R, K, T, Q, max(1, min(R /...  106 us
    unnamed x5, local copies, waits for them, and re-layouts  2.49 us

profile of v3, /device:TPU:7, one launch (start us, length us, event | category | flops | bytes accessed | tf_op | source)
XLA Modules:
  0.0 109.9 jit_solution(17333016848816465220)
XLA Ops:
  0.0 0.7 subtract_add_fusion
  0.7 0.7 iota_compare_fusion
  1.4 0.1 lt.29
  1.5 0.1 copy.6
  1.7 0.1 add.19
  1.8 0.0 copy-start
  1.8 0.9 copy-done
  2.7 0.0 copy-start.1
  2.7 0.8 copy-done.1
  3.6 105.6 %shard_map.55 = bf16[8,16384]{1,0:T(8,128)(2,1)S(1)} custom-call(s32[512]{0:T(512)S(1)} %fusion.1.idx_ref, f32[1,16384]{1,0:T(1,128)S(1)} %copy-done.1, bf16[8,16384]{1,0:T(8,128)(2,1)S(1)} %copy-done, bf16[1,128,4,128,128]{4,3,2,1,0:T(8,128)(2,1)} %w_hbm.1), custom_call_target="tpu_custom_call" | custom-call | tf_op jit(solution)/shard_map/pallas_call | solution.py:175
  109.2 0.7 copy.8
  (1 shorter events, 0.0 us)
Async XLA Ops:
  1.8 1.0 copy-start
  2.7 0.8 copy-start.1
